TPU v7x, 512 devices: a whole 4x8x8 slice. The times are simulated.
512 devices in a mesh: row: 32 (over z, x), rep: 16 (over y, core).
Axes of the slice: x: 4, y: 8, z: 8, core: 2. Of those that a mesh axis runs over, the one named last changes fastest.
Arguments:
- features: bfloat16 [131072, 128], P('row'), may hold values from -6 to 6
- hub_local: int32 [32, 1], P('row'), may hold values from 0 to 31
- send_local: int32 [32, 16, 32, 2], P('row', 'rep'), may hold values from 0 to 31
- tile_rows: int32 [32, 16, 112], P('row', 'rep'), may hold values from 0 to 31
- tile_slots: int32 [32, 16, 112], P('row', 'rep'), may hold values from 0 to 95, as said below
- tile_values: bfloat16 [32, 16, 112, 128, 128], P('row', 'rep'), may hold values from -0.0625 to 0.0625
- weight: bfloat16 [128, 128], replicated, may hold values from -0.5 to 0.5
- out_bias: float32 [128], replicated, may hold values from -3 to 3
Outputs:
- hidden_out: bfloat16 [131072, 128], P(('row', 'rep'))
Inputs may be any that keep to these rules, and one draw needn't show every extreme that they name: For every block and section, each slot of source appears in tile_slots at least once; the last 16 tiles of a section use hub slots.
All inputs are finite; a program needn't handle non-finite values.
Results may differ from a plain program's by a relative error of at most 0.0044.
Values may be sent and summed in bfloat16 or wider, within the bound.
A program may use at most 64 MiB of HBM per device.

v0:
```python
import jax
import jax.numpy as jnp
from jax import lax
from jax.sharding import PartitionSpec as P

F = 128
TILE = 128


def local(features, hub_local, send_local, tile_rows, tile_slots, tile_values, weight, out_bias):
    tile_count = features.shape[0] // TILE
    feature_tiles = features.reshape(tile_count, TILE, F)
    hub_mine = feature_tiles[hub_local[0]]
    hub_all = lax.all_gather(hub_mine, "row", axis=0, tiled=True)
    outgoing = feature_tiles[send_local[0, 0].reshape(-1)]
    received = lax.all_to_all(outgoing, "row", split_axis=0, concat_axis=0, tiled=True)
    source = jnp.concatenate([hub_all, received], axis=0)
    picked = source[tile_slots[0, 0]]
    products = jnp.einsum(
        "kab,kbf->kaf", tile_values[0, 0], picked, preferred_element_type=jnp.float32
    )
    partial_sum = jax.ops.segment_sum(products, tile_rows[0, 0], num_segments=tile_count)
    partial_sum = partial_sum.reshape(tile_count * TILE, F)
    own_rows = lax.psum_scatter(partial_sum, "rep", scatter_dimension=0, tiled=True)
    aggregate = own_rows.astype(jnp.bfloat16)
    mixed = jnp.dot(aggregate, weight, preferred_element_type=jnp.float32) + out_bias
    return jax.nn.relu(mixed).astype(jnp.bfloat16)


def solution(mesh):
    placed = (
        P("row", None),
        P("row", None),
        P("row", "rep", None, None),
        P("row", "rep", None),
        P("row", "rep", None),
        P("row", "rep", None, None, None),
        P(),
        P(),
    )
    return jax.shard_map(
        local, mesh=mesh, in_specs=placed, out_specs=P(("row", "rep"), None), check_vma=False
    )
```

profile of v0, /device:TPU:1, one launch (start us, length us, event | category | flops | bytes accessed | tf_op | source)
XLA Modules:
  0.0 221.9 jit_solution(6122331575191072130)
XLA Ops:
  6.5 0.0 copy-start
  6.5 0.8 copy.14
  7.4 0.1 reshape_squeeze.3
  7.5 0.3 copy-done
  7.8 0.0 copy-start.5
  7.8 2.2 gather_fusion
  9.9 13.7 %all-to-all-start = ((bf16[64,128,128]{2,1,0:T(8,128)(2,1)}), bf16[64,128,128]{2,1,0:T(8,128)(2,1)S(1)}, u32[]{:S(2)}, u32[]{:S(2)}) async-start(bf16[64,128,128]{2,1,0:T(8,128)(2,1)} %gather_fusion), calls=%async_computation | async-start | bytes 4194304 | tf_op jit(solution)/shard_map/all_to_all | solution.py:16
  23.7 0.0 all-gather.2.cloned.1.call-start
  24.4 0.6 constant_dynamic-slice_fusion
  25.0 0.0 all-gather.2.cloned.1.call-update
  25.0 0.0 reduce-scatter.2.cloned.1.call-start
  25.1 0.0 copy-done.5
  25.1 84.5 %all-gather.2.cloned.1.call-done = bf16[32,128,128]{2,1,0:T(8,128)(2,1)} async-done(((bf16[1,128,128]{2,1,0:T(8,128)(2,1)}), bf16[32,128,128]{2,1,0:T(8,128)(2,1)}) %all-gather.2.cloned.1.call-update) | async-done | bytes 1048592 | tf_op jit(solution)/shard_map/all_gather | solution.py:14
  109.6 0.0 all-to-all-done
  109.6 3.1 %pad_maximum_fusion = bf16[96,128,128]{2,1,0:T(8,128)(2,1)} fusion(bf16[64,128,128]{2,1,0:T(8,128)(2,1)S(1)} %all-to-all-done, bf16[32,128,128]{2,1,0:T(8,128)(2,1)} %all-gather.2.cloned.1.call-done), kind=kLoop, calls=%fused_computation.5 | loop fusion | flops 1572864 | bytes 6291456 | tf_op jit(solution)/shard_map/concatenate | solution.py:17
  112.7 4.9 %gather_fusion.1 = bf16[112,128,128]{2,1,0:T(8,128)(2,1)} fusion(bf16[96,128,128]{2,1,0:T(8,128)(2,1)} %pad_maximum_fusion, s32[1024]{0:T(1024)S(1)} %pad_clamp_fusion), kind=kCustom, calls=%fused_computation.1 | custom fusion | bytes 7340480 | tf_op jit(solution)/shard_map/gather | solution.py:18
  117.6 8.8 %fusion.2 = f32[112,128,128]{1,2,0:T(8,128)} fusion(bf16[112,128,128]{2,1,0:T(8,128)(2,1)} %gather_fusion.1, bf16[1,1,112,128,128]{4,3,2,1,0:T(8,128)(2,1)} %param.13), kind=kOutput, calls=%fused_computation.6 | convolution fusion | flops 469762048 | bytes 14680064 | tf_op jit(solution)/shard_map/kab,kbf->kaf/dot_general | solution.py:19
  126.4 0.0 copy-start.3
  126.4 8.6 %copy.16 = f32[112,128,128]{2,1,0:T(8,128)} copy(f32[112,128,128]{1,2,0:T(8,128)} %fusion.2) | data formatting | bytes 14680064 | tf_op jit(solution)/shard_map/kab,kbf->kaf/dot_general | solution.py:19
  135.1 0.2 broadcast_in_dim.4
  135.3 0.0 copy-done.3
  135.3 0.0 copy-start.2
  135.3 0.0 copy-start.4
  135.3 15.0 %scatter_fusion = f32[32,128,128]{2,1,0:T(8,128)S(1)} fusion(f32[32,128,128]{2,1,0:T(8,128)S(1)} %broadcast_in_dim.4, s32[112]{0:T(128)S(1)} %bitcast.28, f32[112,128,128]{2,1,0:T(8,128)} %copy.16), kind=kCustom, calls=%fused_computation.2 | custom fusion | flops 1835008 | bytes 22020544 | tf_op jit(solution)/shard_map/scatter-add | solution.py:22
  150.3 0.0 copy-start.1
  150.3 1.3 copy-done.1
  151.7 0.0 reduce-scatter.2.cloned.1.call-update
  151.7 61.7 %reduce-scatter.2.cloned.1.call-done = f32[256,128]{1,0:T(8,128)} async-done(((f32[4096,128]{1,0:T(8,128)}), f32[256,128]{1,0:T(8,128)}) %reduce-scatter.2.cloned.1.call-update) | async-done | bytes 131088 | tf_op jit(solution)/shard_map/reduce_scatter | solution.py:24
  213.3 0.0 copy-done.2
  213.3 0.0 copy-done.4
  213.3 1.7 fusion.6
  (4 shorter events, 0.0 us)
Async XLA Ops:
  6.5 1.2 copy-start
  7.8 17.3 %copy-start.5 = (s32[1,1,112]{2,1,0:T(1,128)S(1)}, s32[1,1,112]{2,1,0:T(1,128)}, u32[]{:S(2)}) copy-start(s32[1,1,112]{2,1,0:T(1,128)} %param.12) | copy-start | bytes 1348
  9.9 99.7 %all-to-all-start = ((bf16[64,128,128]{2,1,0:T(8,128)(2,1)}), bf16[64,128,128]{2,1,0:T(8,128)(2,1)S(1)}, u32[]{:S(2)}, u32[]{:S(2)}) async-start(bf16[64,128,128]{2,1,0:T(8,128)(2,1)} %gather_fusion), calls=%async_computation | async-start | bytes 4194304 | tf_op jit(solution)/shard_map/all_to_all | solution.py:16
  23.7 86.0 %all-gather.2.cloned.1.call-start = ((), (), s32[]{:S(2)}) async-start(), calls=%async_computation.2 | async-start | bytes 1081344 | tf_op jit(solution)/shard_map/all_gather | solution.py:14
  25.0 188.3 %reduce-scatter.2.cloned.1.call-start = ((), (), s32[]{:S(2)}) async-start(), calls=%async_computation.3 | async-start | bytes 2228224 | tf_op jit(solution)/shard_map/reduce_scatter | solution.py:24
  126.4 8.9 %copy-start.3 = (s32[1,1,112]{2,1,0:T(1,128)S(1)}, s32[1,1,112]{2,1,0:T(1,128)}, u32[]{:S(2)}) copy-start(s32[1,1,112]{2,1,0:T(1,128)} %param.11) | copy-start | bytes 1348
  135.3 78.1 %copy-start.2 = (bf16[128,128]{1,0:T(8,128)(2,1)S(1)}, bf16[128,128]{1,0:T(8,128)(2,1)}, u32[]{:S(2)}) copy-start(bf16[128,128]{1,0:T(8,128)(2,1)} %param.14) | copy-start | bytes 98308
  135.3 78.0 %copy-start.4 = (f32[128]{0:T(128)S(1)}, f32[128]{0:T(128)}, u32[]{:S(2)}) copy-start(f32[128]{0:T(128)} %param.15) | copy-start | bytes 1540
  150.3 1.3 copy-start.1
Sparse Core Ops, SparseCore 0:
  27.7 81.9 all-gather.1
  151.8 61.4 reduce-scatter.1
where the time goes:
time: 224 us; the launch traced here: 222 us
  waiting for transfers between devices  146 us (65%)
  local copies, waits for them, and re-layouts  19.1 us (9%)
  other arithmetic  18.1 us (8%)
  between operations  14.2 us (6%)
  starting transfers between devices  13.8 us (6%)
  matrix products  10.5 us (5%)
    all_gather x1, waiting for transfers between devices, local(): hub_all = lax.all_gather(hub_mine, 'row', axis=0, tiled=True)  84.5 us
    reduce_scatter x1, waiting for transfers between devices, local(): lax.psum_scatter(partial_sum, 'rep', scatter_dimension=0, tiled=True)  61.7 us
    scatter-add x1, other arithmetic, local(): jax.ops.segment_sum(products, tile_rows[0, 0], num_segments=tile_count)  15 us
    all_to_all x1, starting transfers between devices, local(): lax.all_to_all(outgoing, 'row', split_axis=0, concat_axis=0, tiled=True)  13.7 us
    dot_general x1, matrix products, local(): jnp.einsum('kab,kbf->kaf', tile_values[0, 0], picked, preferred_element_t...  8.81 us
    dot_general x1, local copies, waits for them, and re-layouts, local(): jnp.einsum('kab,kbf->kaf', tile_values[0, 0], picked, preferred_element_t...  8.62 us
    gather x1, local copies, waits for them, and re-layouts, local(): picked = source[tile_slots[0, 0]]  4.87 us
  transfers between devices with their start and end apart: 3, of which 2 were waited for; matrix products, arithmetic and copies ran while one was open for 0% of the time, Pallas kernels for 0%

commit v1 on v0

v1 whole, which is shorter than its diff:
```python
import functools

import jax
import jax.numpy as jnp
from jax import lax
from jax.experimental import pallas as pl
from jax.experimental.pallas import tpu as pltpu
from jax.sharding import PartitionSpec as P

F = 128
TILE = 128
NX = 4
NZ = 8
NY = 8
ROWS = 32
HUBS = 32
PIECE = 16
KT = 112
VMEM = pltpu.VMEM
MESH = pl.DeviceIdType.MESH


def zigzag(k, middle):
    return middle + (1 - 2 * (k % 2)) * ((k + 1) // 2)


def exchange_kernel(
    feat, hub, picks, out, outgoing, hub_mine, hub_got,
    hub_send, hub_recv, ring_send, ring_recv, tile_send, tile_recv, own_sem,
):
    r = lax.axis_index("row")
    q = lax.axis_index("rep")
    z, x = r // NX, r % NX
    y, c = q // 2, q % 2

    def partner(i):
        dz, dx = zigzag(i // NX, NZ // 2), zigzag(i % NX, NX // 2)
        return ((z + dz) % NZ) * NX + (x + dx) % NX

    def along_y(d):
        return ((y + d) % NY) * 2 + c

    barrier = pltpu.get_barrier_semaphore()

    def greet_row(i, carry):
        pl.semaphore_signal(barrier, inc=1, device_id=(partner(i), q), device_id_type=MESH)
        return carry

    def greet_y(d, carry):
        pl.semaphore_signal(barrier, inc=1, device_id=(r, along_y(d)), device_id_type=MESH)
        return carry

    lax.fori_loop(0, ROWS - 1, greet_row, 0)
    lax.fori_loop(1, NY, greet_y, 0)

    piece = pl.multiple_of(y * PIECE, PIECE)
    hub_mine[...] = feat[hub[0, 0]]
    hub_got[r] = hub_mine[pl.ds(piece, PIECE), :]
    pl.semaphore_wait(barrier, ROWS - 1 + NY - 1)

    def hub_copy(i):
        return pltpu.make_async_remote_copy(
            src_ref=hub_mine.at[pl.ds(piece, PIECE)], dst_ref=hub_got.at[r],
            send_sem=hub_send.at[i], recv_sem=hub_recv.at[i],
            device_id=(partner(i), q), device_id_type=MESH,
        )

    def tile_copy(i):
        return pltpu.make_async_remote_copy(
            src_ref=outgoing.at[i], dst_ref=out.at[pl.ds(HUBS + 2 * r, 2)],
            send_sem=tile_send.at[i], recv_sem=tile_recv.at[i],
            device_id=(partner(i), q), device_id_type=MESH,
        )

    def ring_copy(d):
        return pltpu.make_async_remote_copy(
            src_ref=hub_got, dst_ref=out.at[pl.ds(0, HUBS), pl.ds(piece, PIECE)],
            send_sem=ring_send.at[d], recv_sem=ring_recv.at[d],
            device_id=(r, along_y(d)), device_id_type=MESH,
        )

    def start_hub(i, carry):
        hub_copy(i).start()
        return carry

    lax.fori_loop(0, ROWS - 1, start_hub, 0)

    def gather(i):
        to = partner(i)
        for j in range(2):
            outgoing[i, j] = feat[picks[0, 0, to * 2 + j]]

    def start_tiles(i, carry):
        gather(i)
        tile_copy(i).start()
        return carry

    lax.fori_loop(0, ROWS - 1, start_tiles, 0)
    gather(ROWS - 1)
    own_tiles = pltpu.make_async_copy(
        outgoing.at[ROWS - 1], out.at[pl.ds(HUBS + 2 * r, 2)], own_sem.at[0]
    )
    own_tiles.start()

    def wait_hub(i, carry):
        hub_copy(i).wait()
        return carry

    lax.fori_loop(0, ROWS - 1, wait_hub, 0)
    own_hub = pltpu.make_async_copy(
        hub_got, out.at[pl.ds(0, HUBS), pl.ds(piece, PIECE)], own_sem.at[1]
    )
    own_hub.start()

    def start_ring(d, carry):
        ring_copy(d).start()
        return carry

    lax.fori_loop(1, NY, start_ring, 0)
    own_tiles.wait()
    own_hub.wait()

    def wait_ring(d, carry):
        ring_copy(d).wait()
        return carry

    lax.fori_loop(1, NY, wait_ring, 0)

    def wait_tiles(i, carry):
        tile_copy(i).wait()
        return carry

    lax.fori_loop(0, ROWS - 1, wait_tiles, 0)


def exchange(features, hub_local, picks):
    return pl.pallas_call(
        exchange_kernel,
        out_shape=jax.ShapeDtypeStruct((HUBS + 2 * ROWS, TILE, F), jnp.bfloat16),
        in_specs=[
            pl.BlockSpec(memory_space=VMEM),
            pl.BlockSpec(memory_space=pltpu.SMEM),
            pl.BlockSpec(memory_space=pltpu.SMEM),
        ],
        out_specs=pl.BlockSpec(memory_space=pl.ANY),
        scratch_shapes=[
            VMEM((ROWS, 2, TILE, F), jnp.bfloat16),
            VMEM((TILE, F), jnp.bfloat16),
            VMEM((ROWS, PIECE, F), jnp.bfloat16),
            pltpu.SemaphoreType.DMA((ROWS,)),
            pltpu.SemaphoreType.DMA((ROWS,)),
            pltpu.SemaphoreType.DMA((NY,)),
            pltpu.SemaphoreType.DMA((NY,)),
            pltpu.SemaphoreType.DMA((ROWS,)),
            pltpu.SemaphoreType.DMA((ROWS,)),
            pltpu.SemaphoreType.DMA((2,)),
        ],
        compiler_params=pltpu.CompilerParams(
            collective_id=0, has_side_effects=True, vmem_limit_bytes=32 * 1024 * 1024
        ),
        name="exchange",
    )(features, hub_local, picks)


STEP = 14


def product_kernel(tile_rows, tile_slots, values, source, total):
    step = pl.program_id(0)

    @pl.when(step == 0)
    def _():
        total[...] = jnp.zeros_like(total)

    for k in range(STEP):
        at = step * STEP + k
        start = pl.multiple_of(tile_rows[at] * TILE, TILE)
        total[pl.ds(start, TILE), :] += jnp.dot(
            values[k], source[tile_slots[at]], preferred_element_type=jnp.float32
        )


def products(tile_rows, tile_slots, values, source):
    return pl.pallas_call(
        product_kernel,
        out_shape=jax.ShapeDtypeStruct((ROWS * TILE, F), jnp.float32),
        grid_spec=pltpu.PrefetchScalarGridSpec(
            num_scalar_prefetch=2,
            grid=(KT // STEP,),
            in_specs=[
                pl.BlockSpec((STEP, TILE, TILE), lambda s, *_: (s, 0, 0)),
                pl.BlockSpec((HUBS + 2 * ROWS, TILE, F), lambda s, *_: (0, 0, 0)),
            ],
            out_specs=pl.BlockSpec((ROWS * TILE, F), lambda s, *_: (0, 0)),
        ),
        compiler_params=pltpu.CompilerParams(vmem_limit_bytes=32 * 1024 * 1024),
        name="products",
    )(tile_rows, tile_slots, values, source)


SHARE = 256


def reduce_kernel(
    part, weight, bias, out, core_got, outgoing, got,
    core_send, core_recv, send_sem, recv_sem,
):
    r = lax.axis_index("row")
    q = lax.axis_index("rep")
    y, c = q // 2, q % 2
    other = 1 - c

    def along_y(d):
        return ((y + d) % NY) * 2 + c

    barrier = pltpu.get_barrier_semaphore()
    pl.semaphore_signal(barrier, inc=1, device_id=(r, y * 2 + other), device_id_type=MESH)
    for d in range(1, NY):
        pl.semaphore_signal(barrier, inc=1, device_id=(r, along_y(d)), device_id_type=MESH)
    pl.semaphore_wait(barrier, NY)

    order = [zigzag(k, NY // 2) for k in range(NY)]
    across = []
    for d in order:
        to = (y + d) % NY
        copy = pltpu.make_async_remote_copy(
            src_ref=part.at[to, other], dst_ref=core_got.at[d],
            send_sem=core_send.at[d], recv_sem=core_recv.at[d],
            device_id=(r, y * 2 + other), device_id_type=MESH,
        )
        copy.start()
        across.append(copy)
    along = []
    for k, d in enumerate(order):
        across[k].wait()
        if d == 0:
            continue
        to = (y + d) % NY
        outgoing[d] = (part[to, c] + core_got[d]).astype(jnp.bfloat16)
        copy = pltpu.make_async_remote_copy(
            src_ref=outgoing.at[d], dst_ref=got.at[d],
            send_sem=send_sem.at[d], recv_sem=recv_sem.at[d],
            device_id=(r, along_y(d)), device_id_type=MESH,
        )
        copy.start()
        along.append(copy)
    total = part[y, c] + core_got[0]
    for copy in along[::-1]:
        copy.wait()
    for d in range(1, NY):
        total = total + got[d].astype(jnp.float32)
    aggregate = total.astype(jnp.bfloat16)
    mixed = jnp.dot(aggregate, weight[...], preferred_element_type=jnp.float32) + bias[...]
    out[...] = jnp.maximum(mixed, 0.0).astype(jnp.bfloat16)


def reduce_rows(part, weight, bias):
    return pl.pallas_call(
        reduce_kernel,
        out_shape=jax.ShapeDtypeStruct((SHARE, F), jnp.bfloat16),
        in_specs=[pl.BlockSpec(memory_space=VMEM)] * 3,
        out_specs=pl.BlockSpec(memory_space=VMEM),
        scratch_shapes=[
            VMEM((NY, SHARE, F), jnp.float32),
            VMEM((NY, SHARE, F), jnp.bfloat16),
            VMEM((NY, SHARE, F), jnp.bfloat16),
            pltpu.SemaphoreType.DMA((NY,)),
            pltpu.SemaphoreType.DMA((NY,)),
            pltpu.SemaphoreType.DMA((NY,)),
            pltpu.SemaphoreType.DMA((NY,)),
        ],
        compiler_params=pltpu.CompilerParams(
            collective_id=1, has_side_effects=True, vmem_limit_bytes=32 * 1024 * 1024
        ),
        name="reduce_rows",
    )(part, weight, bias)


def local(features, hub_local, send_local, tile_rows, tile_slots, tile_values, weight, out_bias):
    source = exchange(features.reshape(ROWS, TILE, F), hub_local, send_local.reshape(1, 1, 2 * ROWS))
    part = products(tile_rows.reshape(KT), tile_slots.reshape(KT), tile_values[0, 0], source)
    return reduce_rows(part.reshape(NY, 2, SHARE, F), weight, out_bias.reshape(1, F))


def solution(mesh):
    placed = (
        P("row", None),
        P("row", None),
        P("row", "rep", None, None),
        P("row", "rep", None),
        P("row", "rep", None),
        P("row", "rep", None, None, None),
        P(),
        P(),
    )
    return jax.shard_map(
        local, mesh=mesh, in_specs=placed, out_specs=P(("row", "rep"), None), check_vma=False
    )
```

time: 224 us -> 93.9 us (0.42)
  waiting for transfers between devices: 146 us -> 0 us
  Pallas kernels: 0 us -> 90.2 us
  other arithmetic: 18.1 us -> 0 us
  local copies, waits for them, and re-layouts: 19.1 us -> 2.74 us
  starting transfers between devices: 13.8 us -> 0 us
  between operations: 14.2 us -> 0.77 us
  matrix products: 10.5 us -> 0 us
    pallas_call x0 -> x3, Pallas kernels: none -> 90.2 us  [the longest x1 68 us: exchange(): pl.pallas_call(exchange_kernel, out_shape=jax.ShapeDtypeStruct((HUBS + 2...]
    all_gather x1 -> x0, waiting for transfers between devices: 84.5 us -> none  [local(): hub_all = lax.all_gather(hub_mine, 'row', axis=0, tiled=True)]
    reduce_scatter x1 -> x0, waiting for transfers between devices: 61.7 us -> none  [local(): lax.psum_scatter(partial_sum, 'rep', scatter_dimension=0, tiled=True)]
    scatter-add x1 -> x0, other arithmetic: 15 us -> none  [local(): jax.ops.segment_sum(products, tile_rows[0, 0], num_segments=tile_count)]
    all_to_all x1 -> x0, starting transfers between devices: 13.7 us -> none  [local(): lax.all_to_all(outgoing, 'row', split_axis=0, concat_axis=0, tiled=True)]
    dot_general x2 -> x0, matrix products: 10.5 us -> none  [the longest x1 8.81 us: local(): jnp.einsum('kab,kbf->kaf', tile_values[0, 0], picked, preferred_element_t...]
    dot_general x1 -> x0, local copies, waits for them, and re-layouts: 8.62 us -> none  [local(): jnp.einsum('kab,kbf->kaf', tile_values[0, 0], picked, preferred_element_t...]
    gather x3 -> x0, local copies, waits for them, and re-layouts: 7.65 us -> none  [the longest x1 4.87 us: local(): picked = source[tile_slots[0, 0]]]
  transfers between devices with their start and end apart: 3 -> 0, of which waited for: 2 -> 0; matrix products, arithmetic and copies ran while one was open for 0% -> 0% of each run, Pallas kernels for 0% -> 0%
where the time goes in v1:
time: 93.9 us; the launch traced here: 93.7 us
  Pallas kernels  90.2 us (96%)
  local copies, waits for them, and re-layouts  2.74 us (3%)
    pallas_call x1, Pallas kernels, exchange(): pl.pallas_call(exchange_kernel, out_shape=jax.ShapeDtypeStruct((HUBS + 2...  68 us
    pallas_call x1, Pallas kernels, reduce_rows(): pl.pallas_call(reduce_kernel, out_shape=jax.ShapeDtypeStruct((SHARE, F),...  19.1 us
    pallas_call x1, Pallas kernels, products(): pl.pallas_call(product_kernel, out_shape=jax.ShapeDtypeStruct((ROWS * TIL...  3.1 us
    unnamed x14, local copies, waits for them, and re-layouts  2.64 us

profile of v1, /device:TPU:1, one launch (start us, length us, event | category | flops | bytes accessed | tf_op | source)
XLA Modules:
  0.0 93.7 jit_solution(18148122496050070538)
XLA Ops:
  0.0 0.0 copy-start.4
  0.0 0.0 copy-start.3
  0.7 0.8 copy.10
  1.4 0.1 reshape.21.picks
  1.6 0.0 copy-start.1
  1.6 1.2 %copy-done.1 = bf16[4096,128]{1,0:T(8,128)(2,1)S(1)} copy-done((bf16[4096,128]{1,0:T(8,128)(2,1)S(1)}, bf16[4096,128]{1,0:T(8,128)(2,1)}, u32[]{:S(2)}) %copy-start.1) | copy-done | bytes 1048600
  2.8 0.0 copy-start
  2.8 68.0 %exchange.1.source = bf16[96,128,128]{2,1,0:T(8,128)(2,1)S(1)} custom-call(bf16[32,128,128]{2,1,0:T(8,128)(2,1)S(1)} %bitcast.10, s32[1,1]{1,0:T(1,128)S(6)} %copy.12.hub, s32[1,1,64]{2,1,0:T(1,128)S(1)} %reshape.21.picks), custom_call_target="tpu_custom_call" | custom-call | tf_op jit(solution)/shard_map/exchange/pallas_call | solution.py:137
  70.7 0.0 copy-done.4
  70.8 0.0 copy-done.3
  70.8 0.0 copy-done
  70.8 0.0 copy-start.2
  70.8 0.0 copy-start.5
  70.8 3.1 %products.1 = f32[4096,128]{1,0:T(8,128)S(1)} custom-call(s32[112]{0:T(128)S(1)} %bitcast.11, s32[112]{0:T(128)S(1)} %bitcast.12, bf16[112,128,128]{2,1,0:T(8,128)(2,1)S(1)} %bitcast.9, bf16[96,128,128]{2,1,0:T(8,128)(2,1)S(1)} %exchange.1.source), custom_call_target="tpu_custom_call" | custom-call | tf_op jit(solution)/shard_map/products/pallas_call | solution.py:184
  73.9 0.0 copy-done.2
  73.9 0.0 copy-done.5
  73.9 19.1 %reduce_rows.1 = bf16[256,128]{1,0:T(8,128)(2,1)S(1)} custom-call(f32[8,2,256,128]{3,2,1,0:T(8,128)S(1)} %bitcast.8, bf16[128,128]{1,0:T(8,128)(2,1)S(1)} %copy-done.2, f32[1,128]{1,0:T(1,128)S(1)} %bitcast.13), custom_call_target="tpu_custom_call" | custom-call | tf_op jit(solution)/shard_map/reduce_rows/pallas_call | solution.py:258
  93.0 0.6 copy.13
Async XLA Ops:
  0.0 70.7 %copy-start.4 = (s32[1,1,112]{2,1,0:T(1,128)S(1)}, s32[1,1,112]{2,1,0:T(1,128)}, u32[]{:S(2)}) copy-start(s32[1,1,112]{2,1,0:T(1,128)} %param.12) | copy-start | bytes 1348
  0.0 70.8 %copy-start.3 = (s32[1,1,112]{2,1,0:T(1,128)S(1)}, s32[1,1,112]{2,1,0:T(1,128)}, u32[]{:S(2)}) copy-start(s32[1,1,112]{2,1,0:T(1,128)} %param.11) | copy-start | bytes 1348
  1.6 1.2 %copy-start.1 = (bf16[4096,128]{1,0:T(8,128)(2,1)S(1)}, bf16[4096,128]{1,0:T(8,128)(2,1)}, u32[]{:S(2)}) copy-start(bf16[4096,128]{1,0:T(8,128)(2,1)} %param.8) | copy-start | bytes 3145732
  2.8 68.0 %copy-start = (bf16[1,1,112,128,128]{4,3,2,1,0:T(8,128)(2,1)S(1)}, bf16[1,1,112,128,128]{4,3,2,1,0:T(8,128)(2,1)}, u32[]{:S(2)}) copy-start(bf16[1,1,112,128,128]{4,3,2,1,0:T(8,128)(2,1)} %param.13) | copy-start | bytes 11010052
  70.8 3.1 %copy-start.2 = (bf16[128,128]{1,0:T(8,128)(2,1)S(1)}, bf16[128,128]{1,0:T(8,128)(2,1)}, u32[]{:S(2)}) copy-start(bf16[128,128]{1,0:T(8,128)(2,1)} %weight.1) | copy-start | bytes 98308
  70.8 3.1 %copy-start.5 = (f32[128]{0:T(128)S(1)}, f32[128]{0:T(128)}, u32[]{:S(2)}) copy-start(f32[128]{0:T(128)} %param.15) | copy-start | bytes 1540

commit v2 on v1

--- a/solution.py
+++ b/solution.py
@@ -24,142 +24,273 @@
     return middle + (1 - 2 * (k % 2)) * ((k + 1) // 2)
 
 
+FAR = (4,)
+NEAR = 28
+CLASS = 16
+HUB_ITEM = len(FAR)
+
+
 def exchange_kernel(
-    feat, hub, picks, out, outgoing, hub_mine, hub_got,
-    hub_send, hub_recv, ring_send, ring_recv, tile_send, tile_recv, own_sem,
+    features, hub, picks, picks_far, out,
+    feat, outgoing, hub_tile, hub_got, far_0, far_out, picks_got, picks_at,
+    feat_sem, own_sem, near_send, near_recv, hub_send, hub_recv, far_send, far_recv,
+    pick_send, pick_recv, pick_sem, ring_send, ring_recv,
+    core_send, core_recv, last_send, last_recv,
 ):
+    far = (far_0,)
     r = lax.axis_index("row")
     q = lax.axis_index("rep")
-    z, x = r // NX, r % NX
-    y, c = q // 2, q % 2
-
-    def partner(i):
-        dz, dx = zigzag(i // NX, NZ // 2), zigzag(i % NX, NX // 2)
-        return ((z + dz) % NZ) * NX + (x + dx) % NX
-
-    def along_y(d):
-        return ((y + d) % NY) * 2 + c
+    z, x = lax.div(r, NX), lax.rem(r, NX)
+    y, c = lax.div(q, 2), lax.rem(q, 2)
+    kind = lax.rem(z + c, 2)
+    half_z = lax.div(z, 2)
+    other = q + 1 - 2 * c
+    layer = [z] + [lax.rem(z + d, NZ) for d in range(1, NZ)]
+    line = [lax.rem(x + d, NX) for d in range(NX)]
+    first_row = [at * NX for at in layer]
+    place = [y] + [lax.rem(y + d, NY) for d in range(1, NY)]
+    shares = [at * 4 + 2 * c for at in place]
+    pieces = [pl.multiple_of(at * PIECE, PIECE) for at in place]
+
+    def remote(src, dst, send, recv, row, rep):
+        return pltpu.make_async_remote_copy(
+            src_ref=src, dst_ref=dst, send_sem=send, recv_sem=recv,
+            device_id=(row, rep), device_id_type=MESH,
+        )
+
+    load = pltpu.make_async_copy(features, feat, feat_sem)
+    load.start()
 
     barrier = pltpu.get_barrier_semaphore()
 
-    def greet_row(i, carry):
-        pl.semaphore_signal(barrier, inc=1, device_id=(partner(i), q), device_id_type=MESH)
-        return carry
-
-    def greet_y(d, carry):
-        pl.semaphore_signal(barrier, inc=1, device_id=(r, along_y(d)), device_id_type=MESH)
-        return carry
-
-    lax.fori_loop(0, ROWS - 1, greet_row, 0)
-    lax.fori_loop(1, NY, greet_y, 0)
-
-    piece = pl.multiple_of(y * PIECE, PIECE)
-    hub_mine[...] = feat[hub[0, 0]]
-    hub_got[r] = hub_mine[pl.ds(piece, PIECE), :]
-    pl.semaphore_wait(barrier, ROWS - 1 + NY - 1)
+    def greet(row, rep):
+        pl.semaphore_signal(barrier, inc=1, device_id=(row, rep), device_id_type=MESH)
+
+    for dz in range(NZ):
+        for dx in range(NX):
+            if dz or dx:
+                greet(first_row[dz] + line[dx], q)
+    for rep in (*(place[d] * 2 + c for d in (1, 2, 6, 7)), other):
+        greet(r, rep)
+
+    load.wait()
+    hub_tile[...] = feat[hub[0, 0]]
+
+    @pl.when(c == 0)
+    def _():
+        hub_got[half_z, x] = hub_tile[pl.ds(pieces[0], PIECE), :]
+
+    pl.semaphore_wait(barrier, ROWS - 1 + 5)
+
+    slot_line, slot_first = lax.div(x, 2), 2 * lax.rem(x, 2)
+
+    def slot(at):
+        return out.at[HUBS // 8 + at, slot_line, pl.ds(slot_first, 2)]
+
+    my_slot = slot(z)
 
     def hub_copy(i):
-        return pltpu.make_async_remote_copy(
-            src_ref=hub_mine.at[pl.ds(piece, PIECE)], dst_ref=hub_got.at[r],
-            send_sem=hub_send.at[i], recv_sem=hub_recv.at[i],
-            device_id=(partner(i), q), device_id_type=MESH,
-        )
-
-    def tile_copy(i):
-        return pltpu.make_async_remote_copy(
-            src_ref=outgoing.at[i], dst_ref=out.at[pl.ds(HUBS + 2 * r, 2)],
-            send_sem=tile_send.at[i], recv_sem=tile_recv.at[i],
-            device_id=(partner(i), q), device_id_type=MESH,
-        )
-
-    def ring_copy(d):
-        return pltpu.make_async_remote_copy(
-            src_ref=hub_got, dst_ref=out.at[pl.ds(0, HUBS), pl.ds(piece, PIECE)],
-            send_sem=ring_send.at[d], recv_sem=ring_recv.at[d],
-            device_id=(r, along_y(d)), device_id_type=MESH,
+        row = lax.rem(z + 2 * lax.div(i, NX) + c, NZ) * NX + lax.rem(x + lax.rem(i, NX), NX)
+        return remote(
+            hub_tile.at[pl.ds(pieces[0], PIECE)], hub_got.at[half_z, x],
+            hub_send.at[i], hub_recv.at[i], row, q,
         )
 
     def start_hub(i, carry):
         hub_copy(i).start()
         return carry
 
-    lax.fori_loop(0, ROWS - 1, start_hub, 0)
-
-    def gather(i):
-        to = partner(i)
-        for j in range(2):
-            outgoing[i, j] = feat[picks[0, 0, to * 2 + j]]
-
-    def start_tiles(i, carry):
-        gather(i)
-        tile_copy(i).start()
-        return carry
-
-    lax.fori_loop(0, ROWS - 1, start_tiles, 0)
-    gather(ROWS - 1)
-    own_tiles = pltpu.make_async_copy(
-        outgoing.at[ROWS - 1], out.at[pl.ds(HUBS + 2 * r, 2)], own_sem.at[0]
-    )
-    own_tiles.start()
-
-    def wait_hub(i, carry):
-        hub_copy(i).wait()
-        return carry
-
-    lax.fori_loop(0, ROWS - 1, wait_hub, 0)
-    own_hub = pltpu.make_async_copy(
-        hub_got, out.at[pl.ds(0, HUBS), pl.ds(piece, PIECE)], own_sem.at[1]
-    )
-    own_hub.start()
-
-    def start_ring(d, carry):
-        ring_copy(d).start()
-        return carry
-
-    lax.fori_loop(1, NY, start_ring, 0)
-    own_tiles.wait()
+    lax.fori_loop(1 - c, CLASS, start_hub, 0)
+    far_copy, pick_copy = [], []
+    for b, dz in enumerate(FAR):
+        far_copy.append(remote(
+            feat.at[pl.ds(shares[0], 2)], far[b].at[pl.ds(shares[0], 2)],
+            far_send.at[b], far_recv.at[b], first_row[dz] + x, q,
+        ))
+        pick_copy.append(remote(
+            picks_far.at[layer[dz]], picks_got.at[b],
+            pick_send.at[b], pick_recv.at[b], first_row[dz] + x, q,
+        ))
+        far_copy[b].start()
+        pick_copy[b].start()
+
+    near_copy = []
+    for dz in (3, 5, 2, 6, 1, 7, 0):
+        for dx in (2, 1, 3, 0):
+            i = len(near_copy)
+            row = first_row[dz] + line[dx]
+            at = row * 2
+            for j in range(2):
+                outgoing[i, j] = feat[picks[0, 0, at + j]]
+            if dz or dx:
+                copy = remote(
+                    outgoing.at[i], my_slot, near_send.at[i], near_recv.at[i], row, q
+                )
+            else:
+                copy = pltpu.make_async_copy(outgoing.at[i], my_slot, own_sem.at[0])
+            copy.start()
+            near_copy.append(copy)
+
+    def chunk(b, dy, first, count):
+        if b == HUB_ITEM:
+            return out.at[pl.ds(2 * first, 2 * count), kind, :, pl.ds(pieces[dy], PIECE)]
+        return far[b].at[pl.ds(shares[dy] + first if first else shares[dy], count)]
+
+    def mine(b):
+        return hub_got if b == HUB_ITEM else chunk(b, 0, 0, 2)
+
+    ring_copies, core_copies = {}, {}
+
+    def start_ring(b, dy, way, first=0, count=2):
+        at = len(ring_copies.setdefault(b, []))
+        copy = remote(
+            chunk(b, dy, first, count) if dy else mine(b), chunk(b, dy, first, count),
+            ring_send.at[b, at], ring_recv.at[b, at], r, place[way % NY] * 2 + c,
+        )
+        copy.start()
+        ring_copies[b].append(copy)
+
+    def start_core(b, dy, first=0, count=2):
+        at = len(core_copies.setdefault(b, []))
+        copy = remote(
+            chunk(b, dy, first, count) if dy else mine(b), chunk(b, dy, first, count),
+            core_send.at[b, at], core_recv.at[b, at], r, other,
+        )
+        copy.start()
+        core_copies[b].append(copy)
+
+    own_hub = pltpu.make_async_copy(hub_got, chunk(HUB_ITEM, 0, 0, 2), own_sem.at[1])
+    to_scalar = [
+        pltpu.make_async_copy(picks_got.at[b], picks_at.at[b], pick_sem.at[b])
+        for b in range(len(FAR))
+    ]
+
+    def spread(b):
+        if b == HUB_ITEM:
+
+            def wait_hub(i, carry):
+                hub_copy(i).wait()
+                return carry
+
+            lax.fori_loop(1 - c, CLASS, wait_hub, 0)
+        else:
+            far_copy[b].wait()
+        for way in (2, -2, 1, -1):
+            start_ring(b, 0, way)
+        start_core(b, 0)
+        if b == HUB_ITEM:
+            own_hub.start()
+        else:
+            pick_copy[b].wait()
+            to_scalar[b].start()
+
+    def spread_on(b):
+        for at, way in enumerate((2, -2)):
+            ring_copies[b][at].wait_recv()
+            on = way // 2
+            start_ring(b, -way % NY, way, 0 if on > 0 else 1, 1)
+            start_ring(b, -way % NY, on)
+            start_core(b, -way % NY)
+        for at, way in ((2, 1), (3, -1)):
+            ring_copies[b][at].wait_recv()
+            start_core(b, -way % NY)
+
+    def collect(b):
+        for at, way in ((5, 3), (7, -3)):
+            ring_copies[b][at].wait_recv()
+            start_core(b, -way % NY)
+        for at, first in ((4, 0), (6, 1)):
+            ring_copies[b][at].wait_recv()
+            start_core(b, NY // 2, first, 1)
+
+    last_copy = []
+
+    def pass_on(b):
+        to_scalar[b].wait()
+        dst = slot(layer[NZ - FAR[b]])
+        for k, dx in enumerate((2, 1, 3, 0)):
+            at = line[dx] * 2
+            for j in range(2):
+                far_out[b, k, j] = far[b][picks_at[b, 0, at + j]]
+            if dx:
+                copy = remote(
+                    far_out.at[b, k], dst, last_send.at[b, k], last_recv.at[b, k],
+                    first_row[0] + line[dx], q,
+                )
+            else:
+                copy = pltpu.make_async_copy(far_out.at[b, k], dst, own_sem.at[2 + b])
+            copy.start()
+            last_copy.append(copy)
+
+    for b in range(len(FAR)):
+        spread(b)
+    spread(HUB_ITEM)
+    for b in range(len(FAR)):
+        spread_on(b)
+    spread_on(HUB_ITEM)
+    for b in range(len(FAR)):
+        collect(b)
+        for copy in core_copies[b]:
+            copy.wait()
+        pass_on(b)
+    collect(HUB_ITEM)
+    for copy in core_copies[HUB_ITEM]:
+        copy.wait()
+
+    for copies in ring_copies.values():
+        for copy in copies:
+            copy.wait_send()
     own_hub.wait()
-
-    def wait_ring(d, carry):
-        ring_copy(d).wait()
-        return carry
-
-    lax.fori_loop(1, NY, wait_ring, 0)
-
-    def wait_tiles(i, carry):
-        tile_copy(i).wait()
-        return carry
-
-    lax.fori_loop(0, ROWS - 1, wait_tiles, 0)
+    for copy in near_copy + last_copy:
+        copy.wait()
 
 
 def exchange(features, hub_local, picks):
+    dma = pltpu.SemaphoreType.DMA
+    far = len(FAR)
+    picks_far = jnp.pad(picks.reshape(NZ, 1, 2 * NX), ((0, 0), (0, 7), (0, 128 - 2 * NX)))
     return pl.pallas_call(
         exchange_kernel,
-        out_shape=jax.ShapeDtypeStruct((HUBS + 2 * ROWS, TILE, F), jnp.bfloat16),
+        out_shape=jax.ShapeDtypeStruct((12, 2, 4, TILE, F), jnp.bfloat16),
         in_specs=[
-            pl.BlockSpec(memory_space=VMEM),
+            pl.BlockSpec(memory_space=pl.ANY),
             pl.BlockSpec(memory_space=pltpu.SMEM),
             pl.BlockSpec(memory_space=pltpu.SMEM),
+            pl.BlockSpec(memory_space=VMEM),
         ],
         out_specs=pl.BlockSpec(memory_space=pl.ANY),
         scratch_shapes=[
-            VMEM((ROWS, 2, TILE, F), jnp.bfloat16),
+            VMEM((ROWS, TILE, F), jnp.bfloat16),
+            VMEM((NEAR, 2, TILE, F), jnp.bfloat16),
             VMEM((TILE, F), jnp.bfloat16),
-            VMEM((ROWS, PIECE, F), jnp.bfloat16),
-            pltpu.SemaphoreType.DMA((ROWS,)),
-            pltpu.SemaphoreType.DMA((ROWS,)),
-            pltpu.SemaphoreType.DMA((NY,)),
-            pltpu.SemaphoreType.DMA((NY,)),
-            pltpu.SemaphoreType.DMA((ROWS,)),
-            pltpu.SemaphoreType.DMA((ROWS,)),
-            pltpu.SemaphoreType.DMA((2,)),
+            VMEM((4, 4, PIECE, F), jnp.bfloat16),
+            *[VMEM((ROWS, TILE, F), jnp.bfloat16)] * far,
+            VMEM((far, NX, 2, TILE, F), jnp.bfloat16),
+            VMEM((far, 8, 128), jnp.int32),
+            pltpu.SMEM((far, 8, 128), jnp.int32),
+            dma(()),
+            dma((2 + far,)),
+            dma((NEAR,)),
+            dma((NEAR,)),
+            dma((CLASS,)),
+            dma((CLASS,)),
+            dma((far,)),
+            dma((far,)),
+            dma((far,)),
+            dma((far,)),
+            dma((far,)),
+            dma((far + 1, 8)),
+            dma((far + 1, 8)),
+            dma((far + 1, 9)),
+            dma((far + 1, 9)),
+            dma((far, NX)),
+            dma((far, NX)),
         ],
         compiler_params=pltpu.CompilerParams(
             collective_id=0, has_side_effects=True, vmem_limit_bytes=32 * 1024 * 1024
         ),
         name="exchange",
-    )(features, hub_local, picks)
+    )(features, hub_local, picks, picks_far)
 
 
 STEP = 14
@@ -278,7 +409,7 @@
 
 def local(features, hub_local, send_local, tile_rows, tile_slots, tile_values, weight, out_bias):
     source = exchange(features.reshape(ROWS, TILE, F), hub_local, send_local.reshape(1, 1, 2 * ROWS))
-    part = products(tile_rows.reshape(KT), tile_slots.reshape(KT), tile_values[0, 0], source)
+    part = products(tile_rows.reshape(KT), tile_slots.reshape(KT), tile_values[0, 0], source.reshape(HUBS + 2 * ROWS, TILE, F))
     return reduce_rows(part.reshape(NY, 2, SHARE, F), weight, out_bias.reshape(1, F))
 
 

time: 93.9 us -> 84.3 us (0.90)
  Pallas kernels: 90.2 us -> 80.4 us
    pallas_call x1, Pallas kernels: 68 us -> 56.4 us  [exchange(): pl.pallas_call(exchange_kernel, out_shape=jax.ShapeDtypeStruct((12, 2, 4,...]
    pallas_call x1, Pallas kernels: 19.1 us -> 21 us  [reduce_rows(): pl.pallas_call(reduce_kernel, out_shape=jax.ShapeDtypeStruct((SHARE, F),...]
where the time goes in v2:
time: 84.3 us; the launch traced here: 84.2 us
  Pallas kernels  80.4 us (95%)
  local copies, waits for them, and re-layouts  2.97 us (4%)
    pallas_call x1, Pallas kernels, exchange(): pl.pallas_call(exchange_kernel, out_shape=jax.ShapeDtypeStruct((12, 2, 4,...  56.4 us
    pallas_call x1, Pallas kernels, reduce_rows(): pl.pallas_call(reduce_kernel, out_shape=jax.ShapeDtypeStruct((SHARE, F),...  21 us
    pallas_call x1, Pallas kernels, products(): pl.pallas_call(product_kernel, out_shape=jax.ShapeDtypeStruct((ROWS * TIL...  3.11 us
    unnamed x14, local copies, waits for them, and re-layouts  2.79 us

profile of v2, /device:TPU:1, one launch (start us, length us, event | category | flops | bytes accessed | tf_op | source)
XLA Modules:
  0.0 84.2 jit_solution(7714900123516251345)
XLA Ops:
  0.0 0.0 copy-start.4
  0.0 0.0 copy-start.3
  0.7 0.8 copy.12
  1.4 0.1 reshape.24.picks
  1.6 0.1 reshape_reshape.3
  1.6 0.0 copy-start
  1.6 0.0 copy-start.1
  1.7 1.4 %copy-done.1 = bf16[4096,128]{1,0:T(8,128)(2,1)S(1)} copy-done((bf16[4096,128]{1,0:T(8,128)(2,1)S(1)}, bf16[4096,128]{1,0:T(8,128)(2,1)}, u32[]{:S(2)}) %copy-start.1) | copy-done | bytes 1048600
  3.0 56.4 %exchange.1 = bf16[12,2,4,128,128]{4,3,2,1,0:T(8,128)(2,1)S(1)} custom-call(bf16[32,128,128]{2,1,0:T(8,128)(2,1)S(1)} %bitcast.15, s32[1,1]{1,0:T(1,128)S(6)} %copy.16.hub, s32[1,1,64]{2,1,0:T(1,128)S(1)} %reshape.24.picks, s32[8,8,128]{2,1,0:T(8,128)S(1)} %pad.4.picks_far), custom_call_target="tpu_custom_call" | custom-call | tf_op jit(solution)/shard_map/exchange/pallas_call | solution.py:252
  59.4 0.0 copy-done.4
  59.4 0.0 copy-done.3
  59.4 0.0 copy-done
  59.4 0.0 copy-start.2
  59.4 0.0 copy-start.5
  59.4 3.1 %products.1 = f32[4096,128]{1,0:T(8,128)S(1)} custom-call(s32[112]{0:T(128)S(1)} %bitcast.16, s32[112]{0:T(128)S(1)} %bitcast.17, bf16[112,128,128]{2,1,0:T(8,128)(2,1)S(1)} %bitcast.14, bf16[96,128,128]{2,1,0:T(8,128)(2,1)S(1)} %bitcast.12), custom_call_target="tpu_custom_call" | custom-call | tf_op jit(solution)/shard_map/products/pallas_call | solution.py:315
  62.5 0.0 copy-done.2
  62.6 0.0 copy-done.5
  62.6 21.0 %reduce_rows.1 = bf16[256,128]{1,0:T(8,128)(2,1)S(1)} custom-call(f32[8,2,256,128]{3,2,1,0:T(8,128)S(1)} %bitcast.13, bf16[128,128]{1,0:T(8,128)(2,1)S(1)} %copy-done.2, f32[1,128]{1,0:T(1,128)S(1)} %bitcast.18), custom_call_target="tpu_custom_call" | custom-call | tf_op jit(solution)/shard_map/reduce_rows/pallas_call | solution.py:389
  83.5 0.6 copy.17
  (1 shorter events, 0.0 us)
Async XLA Ops:
  0.0 59.4 %copy-start.4 = (s32[1,1,112]{2,1,0:T(1,128)S(1)}, s32[1,1,112]{2,1,0:T(1,128)}, u32[]{:S(2)}) copy-start(s32[1,1,112]{2,1,0:T(1,128)} %param.12) | copy-start | bytes 1348
  0.0 59.4 %copy-start.3 = (s32[1,1,112]{2,1,0:T(1,128)S(1)}, s32[1,1,112]{2,1,0:T(1,128)}, u32[]{:S(2)}) copy-start(s32[1,1,112]{2,1,0:T(1,128)} %param.11) | copy-start | bytes 1348
  1.6 57.8 %copy-start = (bf16[1,1,112,128,128]{4,3,2,1,0:T(8,128)(2,1)S(1)}, bf16[1,1,112,128,128]{4,3,2,1,0:T(8,128)(2,1)}, u32[]{:S(2)}) copy-start(bf16[1,1,112,128,128]{4,3,2,1,0:T(8,128)(2,1)} %param.13) | copy-start | bytes 11010052
  1.6 1.4 %copy-start.1 = (bf16[4096,128]{1,0:T(8,128)(2,1)S(1)}, bf16[4096,128]{1,0:T(8,128)(2,1)}, u32[]{:S(2)}) copy-start(bf16[4096,128]{1,0:T(8,128)(2,1)} %param.8) | copy-start | bytes 3145732
  59.4 3.1 %copy-start.2 = (bf16[128,128]{1,0:T(8,128)(2,1)S(1)}, bf16[128,128]{1,0:T(8,128)(2,1)}, u32[]{:S(2)}) copy-start(bf16[128,128]{1,0:T(8,128)(2,1)} %weight.1) | copy-start | bytes 98308
  59.4 3.1 %copy-start.5 = (f32[128]{0:T(128)S(1)}, f32[128]{0:T(128)}, u32[]{:S(2)}) copy-start(f32[128]{0:T(128)} %param.15) | copy-start | bytes 1540

commit v3 on v0

v3 whole, which is shorter than its diff:
```python
import functools

import jax
import jax.numpy as jnp
from jax import lax
from jax.experimental import pallas as pl
from jax.experimental.pallas import tpu as pltpu
from jax.sharding import PartitionSpec as P

F = 128
TILE = 128
NX = 4
NZ = 8
NY = 8
ROWS = 32
HUBS = 32
PIECE = 16
KT = 112
VMEM = pltpu.VMEM
MESH = pl.DeviceIdType.MESH


def zigzag(k, middle):
    return middle + (1 - 2 * (k % 2)) * ((k + 1) // 2)


FAR = 4
NEAR_Z = (3, 5, 2, 6, 1, 7, 0)
LINE = (2, 1, 3, 0)
NEAR = len(NEAR_Z) * NX
CLASS = 16
FAR_ITEM, HUB_ITEM = 0, 1
EMPTY = KT
SHARE = 256
HALF = F // 2
ORDER = tuple(zigzag(k, NY // 2) for k in range(NY))
UNROLL = 8


def halves(one, two):
    return (
        jnp.concatenate([one[:, :HALF], two[:, :HALF]], axis=1),
        jnp.concatenate([one[:, HALF:], two[:, HALF:]], axis=1),
    )


def layer_kernel(
    features, hub, picks, picks_far, rows_at, rows_in, slots, values, weight, bias, out,
    feat, tiles, outgoing, hub_tile, hub_got, far, far_out, picks_got, picks_at,
    source_0, source_1, linked, links, sums, part_own, part_other, core_got, sum_out, sum_got,
    load_sem, scalar_sem, near_send, near_recv, hub_send, hub_recv, far_send, far_recv,
    ring_send, ring_recv, core_send, core_recv, last_send, last_recv,
    cross_send, cross_recv, sum_send, sum_recv,
):
    source = (source_0, source_1)
    r = lax.axis_index("row")
    q = lax.axis_index("rep")
    z, x = lax.div(r, NX), lax.rem(r, NX)
    y, c = lax.div(q, 2), lax.rem(q, 2)
    kind = lax.rem(z + c, 2)
    half_z, odd_z = lax.div(z, 2), lax.rem(z, 2)
    other = q + 1 - 2 * c
    layer = [z] + [lax.rem(z + d, NZ) for d in range(1, NZ)]
    line = [lax.rem(x + d, NX) for d in range(NX)]
    first_row = [at * NX for at in layer]
    place = [y] + [lax.rem(y + d, NY) for d in range(1, NY)]
    shares = [at * 4 + 2 * c for at in place]
    pieces = [pl.multiple_of(at * PIECE, PIECE) for at in place]
    along = [at * 2 + c for at in place]

    def remote(src, dst, send, recv, row, rep):
        return pltpu.make_async_remote_copy(
            src_ref=src, dst_ref=dst, send_sem=send, recv_sem=recv,
            device_id=(row, rep), device_id_type=MESH,
        )

    load = pltpu.make_async_copy(features, feat, load_sem.at[0])
    load.start()
    load_tiles = pltpu.make_async_copy(values, tiles, load_sem.at[1])
    load_tiles.start()

    barrier = pltpu.get_barrier_semaphore()

    def greet(row, rep):
        pl.semaphore_signal(barrier, inc=1, device_id=(row, rep), device_id_type=MESH)

    for dz in range(NZ):
        for dx in range(NX):
            if dz or dx:
                greet(first_row[dz] + line[dx], q)
    for rep in (*along[1:], other):
        greet(r, rep)

    load.wait()
    hub_tile[...] = feat[hub[0, 0]]

    @pl.when(c == 0)
    def _():
        hub_got[half_z, x] = hub_tile[pl.ds(pieces[0], PIECE), :]

    pl.semaphore_wait(barrier, ROWS - 1 + NY)

    def hub_copy(i):
        row = lax.rem(z + 2 * lax.div(i, NX) + c, NZ) * NX + lax.rem(x + lax.rem(i, NX), NX)
        return remote(
            hub_tile.at[pl.ds(pieces[0], PIECE)], hub_got.at[half_z, x],
            hub_send.at[i], hub_recv.at[i], row, q,
        )

    def start_hub(i, carry):
        hub_copy(i).start()
        return carry

    lax.fori_loop(1 - c, CLASS, start_hub, 0)
    far_row = first_row[FAR] + x
    far_copy = remote(
        feat.at[pl.ds(shares[0], 2)], far.at[pl.ds(shares[0], 2)],
        far_send.at[0], far_recv.at[0], far_row, q,
    )
    pick_copy = remote(
        picks_far, picks_got, far_send.at[1], far_recv.at[1], far_row, q
    )
    far_copy.start()
    pick_copy.start()

    near_copy = ([], [])
    for dz in NEAR_Z:
        for dx in LINE:
            i = len(near_copy[0])
            row = first_row[dz] + line[dx]
            pair = halves(feat[picks[0, row]], feat[picks[1, row]])
            if dz == 0 and dx == 0:
                for h in range(2):
                    source[h][4 + half_z, odd_z, x] = pair[h]
                continue
            for h in range(2):
                outgoing[i, h] = pair[h]
                near_copy[h].append(remote(
                    outgoing.at[i, h], source[h].at[4 + half_z, odd_z, x],
                    near_send.at[h, i], near_recv.at[h, i], row, q,
                ))
            near_copy[0][i].start()

    def second_half(first, last):
        for i in range(first, last):
            near_copy[0][i].wait_send()
            near_copy[1][i].start()

    lane = lax.broadcasted_iota(jnp.int32, (1, KT), 1)
    rows_lane = rows_in[...]

    def link(j, carry):
        before, final = carry
        row = rows_at[0, 0, j]
        before = jnp.where((rows_lane == row) & (lane > j), j, before)
        final = jnp.where(lane == row, j, final)
        return before, final

    none = jnp.full((1, KT), EMPTY, jnp.int32)
    before, final = lax.fori_loop(0, KT, link, (none, none))
    linked[...] = jnp.zeros((8, 128), jnp.int32)
    linked[pl.ds(0, 1), pl.ds(0, KT)] = before
    linked[pl.ds(1, 1), pl.ds(0, KT)] = final
    to_links = pltpu.make_async_copy(linked, links, scalar_sem.at[0])
    to_links.start()

    def chunk(b, dy, first, count):
        if b == HUB_ITEM:
            return source_0.at[pl.ds(2 * first, 2 * count), kind, :, pl.ds(pieces[dy], PIECE)]
        return far.at[pl.ds(shares[dy] + first if first else shares[dy], count)]

    def mine(b):
        return hub_got if b == HUB_ITEM else chunk(b, 0, 0, 2)

    ring_copies, core_copies = ([], []), ([], [])

    def start_ring(b, dy, way, first=0, count=2):
        at = len(ring_copies[b])
        copy = remote(
            chunk(b, dy, first, count) if dy else mine(b), chunk(b, dy, first, count),
            ring_send.at[b, at], ring_recv.at[b, at], r, along[way % NY],
        )
        copy.start()
        ring_copies[b].append(copy)

    def start_core(b, dy, first=0, count=2):
        at = len(core_copies[b])
        copy = remote(
            chunk(b, dy, first, count) if dy else mine(b), chunk(b, dy, first, count),
            core_send.at[b, at], core_recv.at[b, at], r, other,
        )
        copy.start()
        core_copies[b].append(copy)

    own_hub = pltpu.make_async_copy(hub_got, chunk(HUB_ITEM, 0, 0, 2), load_sem.at[2])
    to_scalar = pltpu.make_async_copy(picks_got, picks_at, scalar_sem.at[1])

    def spread(b):
        if b == HUB_ITEM:

            def wait_hub(i, carry):
                hub_copy(i).wait()
                return carry

            lax.fori_loop(1 - c, CLASS, wait_hub, 0)
        else:
            far_copy.wait()
        for way in (2, -2, 1, -1):
            start_ring(b, 0, way)
        start_core(b, 0)
        if b == HUB_ITEM:
            own_hub.start()
        else:
            pick_copy.wait()
            to_scalar.start()

    def spread_on(b):
        for at, way in enumerate((2, -2)):
            ring_copies[b][at].wait_recv()
            on = way // 2
            start_ring(b, -way % NY, way, 0 if on > 0 else 1, 1)
            start_ring(b, -way % NY, on)
            start_core(b, -way % NY)
        for at, way in ((2, 1), (3, -1)):
            ring_copies[b][at].wait_recv()
            start_core(b, -way % NY)

    def collect(b):
        for at, way in ((5, 3), (7, -3)):
            ring_copies[b][at].wait_recv()
            start_core(b, -way % NY)
        for at, first in ((4, 0), (6, 1)):
            ring_copies[b][at].wait_recv()
            start_core(b, NY // 2, first, 1)
        for copy in core_copies[b]:
            copy.wait()

    last_copy = ([], [])

    def pass_on():
        to_scalar.wait()
        z_from = layer[NZ - FAR]
        group, odd = lax.div(z_from, 2), lax.rem(z_from, 2)
        for k, dx in enumerate(LINE):
            at = first_row[0] + line[dx]
            pair = halves(far[picks_at[0, at]], far[picks_at[1, at]])
            for h in range(2):
                if dx == 0:
                    source[h][4 + group, odd, x] = pair[h]
                    continue
                far_out[h, k] = pair[h]
                last_copy[h].append(remote(
                    far_out.at[h, k], source[h].at[4 + group, odd, x],
                    last_send.at[h, k], last_recv.at[h, k], first_row[0] + line[dx], q,
                ))
        for h in range(2):
            for copy in last_copy[h]:
                copy.start()

    spread(FAR_ITEM)
    spread(HUB_ITEM)
    second_half(0, 6)
    spread_on(FAR_ITEM)
    spread_on(HUB_ITEM)
    second_half(6, 14)
    collect(FAR_ITEM)
    pass_on()
    collect(HUB_ITEM)
    own_hub.wait()
    second_half(14, NEAR - 1)
    to_links.wait()
    load_tiles.wait()
    sums[EMPTY] = jnp.zeros((TILE, F), jnp.float32)
    source_1[pl.ds(0, 4)] = source_0[pl.ds(0, 4)]

    left = lax.broadcasted_iota(jnp.int32, (TILE, F), 1) < HALF

    def products(h):
        def step(n, carry):
            for u in range(UNROLL):
                k = n * UNROLL + u
                at = slots[0, 0, k]
                is_hub = at < HUBS
                tile = jnp.where(is_hub, at, lax.div(at + HUBS, 2))
                side = jnp.where(is_hub, h, lax.rem(at, 2))
                product = jnp.dot(
                    tiles[k],
                    source[h][lax.div(tile, 8), lax.rem(lax.div(tile, 4), 2), lax.rem(tile, 4)],
                    preferred_element_type=jnp.float32,
                )
                turned = jnp.concatenate([product[:, HALF:], product[:, :HALF]], axis=1)
                same = side == lax.rem(rows_at[0, 0, k], 2)
                sums[k] = sums[links[0, k]] + jnp.where(same, product, turned)
            return carry

        lax.fori_loop(0, KT // UNROLL, step, 0)

    cross_copy = ([], [])
    sum_copy = ([], [])

    def start_sums(h):
        def packed(rep):
            at = rep * 2
            return jnp.where(left, sums[links[1, at]], sums[links[1, at + 1]])

        for dy in ORDER:
            part_other[h, dy] = packed(along[dy] + 1 - 2 * c)
            copy = remote(
                part_other.at[h, dy], core_got.at[h, dy],
                cross_send.at[h, dy], cross_recv.at[h, dy], r, other,
            )
            copy.start()
            cross_copy[h].append(copy)
            part_own[h, dy] = packed(along[dy])
        for k, dy in enumerate(ORDER):
            cross_copy[h][k].wait_recv()
            if dy == 0:
                continue
            sum_out[h, dy] = (part_own[h, dy] + core_got[h, dy]).astype(jnp.bfloat16)
            copy = remote(
                sum_out.at[h, dy], sum_got.at[h, dy],
                sum_send.at[h, dy], sum_recv.at[h, dy], r, along[dy],
            )
            copy.start()
            sum_copy[h].append(copy)

    for h in range(2):
        for copy in near_copy[h] + last_copy[h]:
            copy.wait_recv()
        products(h)
        start_sums(h)

    totals = []
    for h in range(2):
        total = part_own[h, 0] + core_got[h, 0]
        for copy in sum_copy[h]:
            copy.wait_recv()
        for dy in range(1, NY):
            total = total + sum_got[h, dy].astype(jnp.float32)
        totals.append(total)
    for t, rows in enumerate(halves(*totals)):
        mixed = jnp.dot(rows.astype(jnp.bfloat16), weight[...], preferred_element_type=jnp.float32)
        out[pl.ds(t * TILE, TILE), :] = jnp.maximum(mixed + bias[...], 0.0).astype(jnp.bfloat16)

    for copy in [*near_copy[1], *ring_copies[0], *ring_copies[1], *last_copy[0], *last_copy[1]]:
        copy.wait_send()
    for copy in [*cross_copy[0], *cross_copy[1], *sum_copy[0], *sum_copy[1]]:
        copy.wait_send()


def local(features, hub_local, send_local, tile_rows, tile_slots, tile_values, weight, out_bias):
    dma = pltpu.SemaphoreType.DMA
    smem, vmem, anywhere = (
        pl.BlockSpec(memory_space=space) for space in (pltpu.SMEM, VMEM, pl.ANY)
    )
    bf16, f32, i32 = jnp.bfloat16, jnp.float32, jnp.int32
    picks = send_local[0, 0].T
    rows_in = tile_rows.reshape(1, KT)
    return pl.pallas_call(
        layer_kernel,
        out_shape=jax.ShapeDtypeStruct((SHARE, F), bf16),
        in_specs=[anywhere, smem, smem, vmem, smem, vmem, smem, anywhere, vmem, vmem],
        out_specs=vmem,
        scratch_shapes=[
            VMEM((ROWS, TILE, F), bf16),
            VMEM((KT, TILE, TILE), bf16),
            VMEM((NEAR, 2, TILE, F), bf16),
            VMEM((TILE, F), bf16),
            VMEM((4, 4, PIECE, F), bf16),
            VMEM((ROWS, TILE, F), bf16),
            VMEM((2, NX, TILE, F), bf16),
            VMEM((2, ROWS), i32),
            pltpu.SMEM((2, ROWS), i32),
            VMEM((8, 2, 4, TILE, F), bf16),
            VMEM((8, 2, 4, TILE, F), bf16),
            VMEM((8, 128), i32),
            pltpu.SMEM((8, 128), i32),
            VMEM((KT + 1, TILE, F), f32),
            VMEM((2, NY, TILE, F), f32),
            VMEM((2, NY, TILE, F), f32),
            VMEM((2, NY, TILE, F), f32),
            VMEM((2, NY, TILE, F), bf16),
            VMEM((2, NY, TILE, F), bf16),
            dma((3,)),
            dma((2,)),
            dma((2, NEAR)),
            dma((2, NEAR)),
            dma((CLASS,)),
            dma((CLASS,)),
            dma((2,)),
            dma((2,)),
            dma((2, 8)),
            dma((2, 8)),
            dma((2, 9)),
            dma((2, 9)),
            dma((2, NX)),
            dma((2, NX)),
            dma((2, NY)),
            dma((2, NY)),
            dma((2, NY)),
            dma((2, NY)),
        ],
        compiler_params=pltpu.CompilerParams(
            collective_id=0, has_side_effects=True, vmem_limit_bytes=56 * 1024 * 1024
        ),
        name="layer",
    )(
        features.reshape(ROWS, TILE, F), hub_local, picks, picks, tile_rows, rows_in,
        tile_slots, tile_values[0, 0], weight, out_bias.reshape(1, F),
    )


def solution(mesh):
    placed = (
        P("row", None),
        P("row", None),
        P("row", "rep", None, None),
        P("row", "rep", None),
        P("row", "rep", None),
        P("row", "rep", None, None, None),
        P(),
        P(),
    )
    return jax.shard_map(
        local, mesh=mesh, in_specs=placed, out_specs=P(("row", "rep"), None), check_vma=False
    )
```

time: 224 us -> 77.1 us (0.34)
  waiting for transfers between devices: 146 us -> 0 us
  Pallas kernels: 0 us -> 74.7 us
  other arithmetic: 18.1 us -> 0 us
  local copies, waits for them, and re-layouts: 19.1 us -> 1.47 us
  starting transfers between devices: 13.8 us -> 0 us
  between operations: 14.2 us -> 0.66 us
  matrix products: 10.5 us -> 0 us
    all_gather x1 -> x0, waiting for transfers between devices: 84.5 us -> none  [local(): hub_all = lax.all_gather(hub_mine, 'row', axis=0, tiled=True)]
    pallas_call x0 -> x1, Pallas kernels: none -> 74.7 us  [local(): pl.pallas_call(layer_kernel, out_shape=jax.ShapeDtypeStruct((SHARE, F), b...]
    reduce_scatter x1 -> x0, waiting for transfers between devices: 61.7 us -> none  [local(): lax.psum_scatter(partial_sum, 'rep', scatter_dimension=0, tiled=True)]
    scatter-add x1 -> x0, other arithmetic: 15 us -> none  [local(): jax.ops.segment_sum(products, tile_rows[0, 0], num_segments=tile_count)]
    all_to_all x1 -> x0, starting transfers between devices: 13.7 us -> none  [local(): lax.all_to_all(outgoing, 'row', split_axis=0, concat_axis=0, tiled=True)]
    dot_general x2 -> x0, matrix products: 10.5 us -> none  [the longest x1 8.81 us: local(): jnp.einsum('kab,kbf->kaf', tile_values[0, 0], picked, preferred_element_t...]
    dot_general x1 -> x0, local copies, waits for them, and re-layouts: 8.62 us -> none  [local(): jnp.einsum('kab,kbf->kaf', tile_values[0, 0], picked, preferred_element_t...]
    gather x3 -> x0, local copies, waits for them, and re-layouts: 7.65 us -> none  [the longest x1 4.87 us: local(): picked = source[tile_slots[0, 0]]]
  transfers between devices with their start and end apart: 3 -> 0, of which waited for: 2 -> 0; matrix products, arithmetic and copies ran while one was open for 0% -> 0% of each run, Pallas kernels for 0% -> 0%
where the time goes in v3:
time: 77.1 us; the launch traced here: 76.9 us
  Pallas kernels  74.7 us (97%)
  local copies, waits for them, and re-layouts  1.47 us (2%)
    pallas_call x1, Pallas kernels, local(): pl.pallas_call(layer_kernel, out_shape=jax.ShapeDtypeStruct((SHARE, F), b...  74.7 us

profile of v3, /device:TPU:1, one launch (start us, length us, event | category | flops | bytes accessed | tf_op | source)
XLA Modules:
  0.0 76.9 jit_solution(4711632720685212135)
XLA Ops:
  0.7 74.7 %layer.1 = bf16[256,128]{1,0:T(8,128)(2,1)} custom-call(bf16[32,128,128]{2,1,0:T(8,128)(2,1)} %bitcast.8, s32[1,1]{1,0:T(1,128)S(6)} %copy.10.hub, s32[2,32]{1,0:T(2,128)} %bitcast.9, s32[2,32]{1,0:T(2,128)} %bitcast.10, s32[1,1,112]{2,1,0:T(1,128)} %rows_at.1, s32[1,112]{1,0:T(1,128)} %bitcast.11, s32[1,1,112]{2,1,0:T(1,128)} %slots.1, ...), custom_call_target="tpu_custom_call" | custom-call | tf_op jit(solution)/shard_map/layer/pallas_call | solution.py:359
  75.4 1.5 %copy.11 = bf16[256,128]{1,0:T(8,128)(2,1)} copy(bf16[256,128]{1,0:T(8,128)(2,1)} %layer.1) | data formatting | bytes 131072

commit v4 on v3

v4 whole, which is shorter than its diff:
```python
import functools

import jax
import jax.numpy as jnp
from jax import lax
from jax.experimental import pallas as pl
from jax.experimental.pallas import tpu as pltpu
from jax.sharding import PartitionSpec as P

F = 128
TILE = 128
NX = 4
NZ = 8
NY = 8
ROWS = 32
HUBS = 32
PIECE = 16
KT = 112
VMEM = pltpu.VMEM
MESH = pl.DeviceIdType.MESH


def zigzag(k, middle):
    return middle + (1 - 2 * (k % 2)) * ((k + 1) // 2)


FAR = (4, 3, 5)
LINE = (2, 1, 3, 0)
CLASS = 16
HUB_ITEM = len(FAR)
EMPTY = KT
SHARE = 256
HALF = F // 2
ORDER = tuple(zigzag(k, NY // 2) for k in range(NY))
UNROLL = 28


def halves(one, two):
    return (
        jnp.concatenate([one[:, :HALF], two[:, :HALF]], axis=1),
        jnp.concatenate([one[:, HALF:], two[:, HALF:]], axis=1),
    )


def layer_kernel(
    features, hub_in, picks_in, rows_in, slots_in, values, weight_in, bias_in, out,
    hub, picks, rows_at, rows_lane, slots, weight, bias, feat, tiles, out_0, out_1, hub_tile, hub_got, far_mine, far_0, far_1, far_2, far_out, picks_got, picks_at,
    source_0, source_1, linked, links, sums, part_own, part_other, core_got, sum_out, sum_got,
    load_sem, scalar_sem, near_send, near_recv, hub_send, hub_recv, far_send, far_recv,
    pick_send, pick_recv, ring_send, ring_recv, core_send, core_recv, last_send, last_recv,
    cross_send, cross_recv, sum_send, sum_recv,
):
    source = (source_0, source_1)
    far = (far_0, far_1, far_2)
    near_out = (out_0, out_1)
    r = lax.axis_index("row")
    q = lax.axis_index("rep")
    z, x = lax.div(r, NX), lax.rem(r, NX)
    y, c = lax.div(q, 2), lax.rem(q, 2)
    kind = lax.rem(z + c, 2)
    half_z, odd_z = lax.div(z, 2), lax.rem(z, 2)
    other = q + 1 - 2 * c
    layer = [z] + [lax.rem(z + d, NZ) for d in range(1, NZ)]
    line = [lax.rem(x + d, NX) for d in range(NX)]
    first_row = [at * NX for at in layer]
    place = [y] + [lax.rem(y + d, NY) for d in range(1, NY)]
    shares = [at * 2 + c for at in place]
    pieces = [pl.multiple_of(at * PIECE, PIECE) for at in place]
    along = [at * 2 + c for at in place]

    def remote(src, dst, send, recv, row, rep):
        return pltpu.make_async_remote_copy(
            src_ref=src, dst_ref=dst, send_sem=send, recv_sem=recv,
            device_id=(row, rep), device_id_type=MESH,
        )

    loads = {}
    for n, (name, src, dst) in enumerate((
        ("hub", hub_in, hub),
        ("picks", picks_in, picks),
        ("feat", features, feat),
        ("rows", rows_in, rows_at),
        ("lane", rows_in, rows_lane),
        ("slots", slots_in, slots),
        ("weight", weight_in, weight),
        ("bias", bias_in, bias),
        ("tiles", values, tiles),
    )):
        loads[name] = pltpu.make_async_copy(src, dst, load_sem.at[1 + n])
        loads[name].start()

    barrier = pltpu.get_barrier_semaphore()

    def greet(row, rep):
        pl.semaphore_signal(barrier, inc=1, device_id=(row, rep), device_id_type=MESH)

    for dz in range(NZ):
        for dx in range(NX):
            if dz or dx:
                greet(first_row[dz] + line[dx], q)
    for rep in (*along[1:], other):
        greet(r, rep)

    pl.semaphore_wait(barrier, ROWS - 1 + NY)

    for name in ("hub", "picks", "feat"):
        loads[name].wait()
    far_mine[...] = halves(feat[2 * shares[0]], feat[2 * shares[0] + 1])[1]
    far_copy, pick_copy = [], []
    for b, dz in enumerate(FAR):
        to = first_row[dz] + x
        far_copy.append(remote(
            far_mine, far[b].at[shares[0]], far_send.at[b], far_recv.at[b], to, q
        ))
        pick_copy.append(remote(
            picks_in, picks_got.at[b], pick_send.at[b], pick_recv.at[b], to, q
        ))
        far_copy[b].start()
        pick_copy[b].start()
    hub_tile[...] = feat[hub[0, 0]]

    @pl.when(c == 0)
    def _():
        hub_got[half_z, x] = hub_tile[pl.ds(pieces[0], PIECE), :]

    def hub_copy(i):
        row = lax.rem(z + 2 * lax.div(i, NX) + c, NZ) * NX + lax.rem(x + lax.rem(i, NX), NX)
        return remote(
            hub_tile.at[pl.ds(pieces[0], PIECE)], hub_got.at[half_z, x],
            hub_send.at[i], hub_recv.at[i], row, q,
        )

    def start_hub(i, carry):
        hub_copy(i).start()
        return carry

    lax.fori_loop(1 - c, CLASS, start_hub, 0)
    near_copy = ([], [])

    def first_half(dz):
        for dx in LINE:
            row = first_row[dz] + line[dx]
            pair = halves(feat[picks[0, row]], feat[picks[1, row]])
            for h in range(1 if dz in FAR else 2):
                at = source[h].at[4 + half_z, odd_z, x]
                if dz == 0 and dx == 0:
                    at[...] = pair[h]
                    continue
                i = len(near_copy[h])
                near_out[h][i] = pair[h]
                near_copy[h].append(remote(
                    near_out[h].at[i], at, near_send.at[h, i], near_recv.at[h, i], row, q
                ))
                if h == 0:
                    near_copy[0][i].start()

    def second_half(first, last):
        for i in range(first, last):
            near_copy[1][i].start()

    def chunk(b, dy, part):
        if b == HUB_ITEM:
            groups = (pl.ds(0, 4), pl.ds(0, 2), pl.ds(2, 2))[part]
            return source_0.at[groups, kind, :, pl.ds(pieces[dy], PIECE)]
        return far[b].at[shares[dy], (pl.ds(0, TILE), pl.ds(0, HALF), pl.ds(HALF, HALF))[part]]

    def mine(b):
        return hub_got if b == HUB_ITEM else chunk(b, 0, 0)

    ring_copies = [[] for _ in range(HUB_ITEM + 1)]
    core_copies = [[] for _ in range(HUB_ITEM + 1)]

    def start_ring(b, dy, way, part=0):
        at = len(ring_copies[b])
        copy = remote(
            chunk(b, dy, part) if dy else mine(b), chunk(b, dy, part),
            ring_send.at[b, at], ring_recv.at[b, at], r, along[way % NY],
        )
        copy.start()
        ring_copies[b].append(copy)

    def start_core(b, dy, part=0):
        at = len(core_copies[b])
        copy = remote(
            chunk(b, dy, part) if dy else mine(b), chunk(b, dy, part),
            core_send.at[b, at], core_recv.at[b, at], r, other,
        )
        copy.start()
        core_copies[b].append(copy)

    own_hub = pltpu.make_async_copy(hub_got, chunk(HUB_ITEM, 0, 0), load_sem.at[0])
    to_scalar = [
        pltpu.make_async_copy(picks_got.at[b], picks_at.at[b], scalar_sem.at[1 + b])
        for b in range(HUB_ITEM)
    ]

    def spread(b):
        if b == HUB_ITEM:

            def wait_hub(i, carry):
                hub_copy(i).wait()
                return carry

            lax.fori_loop(1 - c, CLASS, wait_hub, 0)
        else:
            far_copy[b].wait()
        for way in (2, -2, 1, -1):
            start_ring(b, 0, way)
        start_core(b, 0)
        if b == HUB_ITEM:
            own_hub.start()
        else:
            pick_copy[b].wait()
            to_scalar[b].start()

    def spread_on(b):
        for at, way in enumerate((2, -2)):
            ring_copies[b][at].wait_recv()
            on = way // 2
            start_ring(b, -way % NY, way, 1 if on > 0 else 2)
            start_ring(b, -way % NY, on)
            start_core(b, -way % NY)
        for at, way in ((2, 1), (3, -1)):
            ring_copies[b][at].wait_recv()
            start_core(b, -way % NY)

    def collect(b):
        for at, way in ((5, 3), (7, -3)):
            ring_copies[b][at].wait_recv()
            start_core(b, -way % NY)
        for at, part in ((4, 1), (6, 2)):
            ring_copies[b][at].wait_recv()
            start_core(b, NY // 2, part)
        for copy in core_copies[b]:
            copy.wait()

    last_copy = []

    def pass_on(b):
        to_scalar[b].wait()
        z_from = layer[NZ - FAR[b]]
        at = source_1.at[4 + lax.div(z_from, 2), lax.rem(z_from, 2), x]
        for k, dx in enumerate(LINE):
            row = first_row[0] + line[dx]
            sides = []
            for j in range(2):
                pick = picks_at[b, j, row]
                pair = far[b][lax.div(pick, 2)]
                turned = jnp.concatenate([pair[:, HALF:], pair[:, :HALF]], axis=1)
                sides.append(jnp.where(lax.rem(pick, 2) == j, pair, turned))
            both = jnp.concatenate([sides[0][:, :HALF], sides[1][:, HALF:]], axis=1)
            if dx == 0:
                at[...] = both
                continue
            far_out[b, k] = both
            copy = remote(
                far_out.at[b, k], at, last_send.at[b, k], last_recv.at[b, k], row, q
            )
            copy.start()
            last_copy.append(copy)

    first_half(2)
    first_half(6)
    spread(0)
    first_half(4)
    spread(HUB_ITEM)
    spread(1)
    spread(2)
    first_half(3)
    first_half(5)
    spread_on(0)
    spread_on(HUB_ITEM)
    first_half(1)
    first_half(7)
    first_half(0)
    spread_on(1)
    spread_on(2)
    second_half(0, len(near_copy[1]))
    collect(0)
    pass_on(0)
    collect(HUB_ITEM)
    own_hub.wait()

    lane = lax.broadcasted_iota(jnp.int32, (1, KT), 1)
    loads["rows"].wait()
    loads["lane"].wait()
    rows = rows_lane[...]

    def link(j, carry):
        before, final = carry
        row = rows_at[0, j]
        before = jnp.where((rows == row) & (lane > j), j, before)
        final = jnp.where(lane == row, j, final)
        return before, final

    none = jnp.full((1, KT), EMPTY, jnp.int32)
    before, final = lax.fori_loop(0, KT, link, (none, none))
    linked[...] = jnp.zeros((8, 128), jnp.int32)
    linked[pl.ds(0, 1), pl.ds(0, KT)] = before
    linked[pl.ds(1, 1), pl.ds(0, KT)] = final
    to_links = pltpu.make_async_copy(linked, links, scalar_sem.at[0])
    to_links.start()

    for b in (1, 2):
        collect(b)
        pass_on(b)
    to_links.wait()
    loads["slots"].wait()
    loads["tiles"].wait()
    sums[EMPTY] = jnp.zeros((TILE, F), jnp.float32)
    source_1[pl.ds(0, 4)] = source_0[pl.ds(0, 4)]

    left = lax.broadcasted_iota(jnp.int32, (TILE, F), 1) < HALF

    def products(h):
        def step(n, carry):
            for u in range(UNROLL):
                k = n * UNROLL + u
                at = slots[0, k]
                is_hub = at < HUBS
                tile = jnp.where(is_hub, at, lax.div(at + HUBS, 2))
                side = jnp.where(is_hub, h, lax.rem(at, 2))
                picked = source[h][lax.div(tile, 8), lax.rem(lax.div(tile, 4), 2), lax.rem(tile, 4)]
                turned = jnp.concatenate([picked[:, HALF:], picked[:, :HALF]], axis=1)
                same = side == lax.rem(rows_at[0, k], 2)
                sums[k] = sums[links[0, k]] + jnp.dot(
                    tiles[k], jnp.where(same, picked, turned), preferred_element_type=jnp.float32
                )
            return carry

        lax.fori_loop(0, KT // UNROLL, step, 0)

    cross_copy = ([], [])
    sum_copy = ([], [])

    def start_sums(h):
        def packed(rep):
            at = rep * 2
            return jnp.where(left, sums[links[1, at]], sums[links[1, at + 1]])

        for dy in ORDER:
            part_other[h, dy] = packed(along[dy] + 1 - 2 * c)
            copy = remote(
                part_other.at[h, dy], core_got.at[h, dy],
                cross_send.at[h, dy], cross_recv.at[h, dy], r, other,
            )
            copy.start()
            cross_copy[h].append(copy)
        for k, dy in enumerate(ORDER):
            own = packed(along[dy])
            cross_copy[h][k].wait_recv()
            if dy == 0:
                part_own[h] = own + core_got[h, dy]
                continue
            sum_out[h, dy] = (own + core_got[h, dy]).astype(jnp.bfloat16)
            copy = remote(
                sum_out.at[h, dy], sum_got.at[h, dy],
                sum_send.at[h, dy], sum_recv.at[h, dy], r, along[dy],
            )
            copy.start()
            sum_copy[h].append(copy)

    for h in range(2):
        for copy in near_copy[h] + (last_copy if h else []):
            copy.wait_recv()
        products(h)
        start_sums(h)

    totals = []
    loads["weight"].wait()
    loads["bias"].wait()
    for h in range(2):
        total = part_own[h]
        for copy, dy in zip(sum_copy[h], ORDER):
            copy.wait_recv()
            total = total + sum_got[h, dy].astype(jnp.float32)
        totals.append(total)
    for t, rows in enumerate(halves(*totals)):
        mixed = jnp.dot(rows.astype(jnp.bfloat16), weight[...], preferred_element_type=jnp.float32)
        out[pl.ds(t * TILE, TILE), :] = jnp.maximum(mixed + bias[...], 0.0).astype(jnp.bfloat16)

    for copy in [*near_copy[0], *near_copy[1], *last_copy]:
        copy.wait_send()
    for copies in ring_copies:
        for copy in copies:
            copy.wait_send()
    for copy in [*cross_copy[0], *cross_copy[1], *sum_copy[0], *sum_copy[1]]:
        copy.wait_send()


def local(features, hub_local, send_local, tile_rows, tile_slots, tile_values, weight, out_bias):
    dma = pltpu.SemaphoreType.DMA
    bf16, f32, i32 = jnp.bfloat16, jnp.float32, jnp.int32
    picks = send_local[0, 0].T
    rows_in = tile_rows.reshape(1, KT)
    return pl.pallas_call(
        layer_kernel,
        out_shape=jax.ShapeDtypeStruct((SHARE, F), bf16),
        in_specs=[pl.BlockSpec(memory_space=pltpu.HBM)] * 8,
        out_specs=pl.BlockSpec(memory_space=VMEM),
        scratch_shapes=[
            pltpu.SMEM((1, 1), i32),
            pltpu.SMEM((2, ROWS), i32),
            pltpu.SMEM((1, KT), i32),
            VMEM((1, KT), i32),
            pltpu.SMEM((1, KT), i32),
            VMEM((F, F), bf16),
            VMEM((1, F), f32),
            VMEM((ROWS, TILE, F), bf16),
            VMEM((KT, TILE, TILE), bf16),
            VMEM((ROWS - 1, TILE, F), bf16),
            VMEM((ROWS - 1, TILE, F), bf16),
            VMEM((TILE, F), bf16),
            VMEM((4, 4, PIECE, F), bf16),
            VMEM((TILE, F), bf16),
            *[VMEM((ROWS // 2, TILE, F), bf16)] * HUB_ITEM,
            VMEM((HUB_ITEM, NX, TILE, F), bf16),
            VMEM((HUB_ITEM, 2, ROWS), i32),
            pltpu.SMEM((HUB_ITEM, 2, ROWS), i32),
            VMEM((8, 2, 4, TILE, F), bf16),
            VMEM((8, 2, 4, TILE, F), bf16),
            VMEM((8, 128), i32),
            pltpu.SMEM((8, 128), i32),
            VMEM((KT + 1, TILE, F), f32),
            VMEM((2, TILE, F), f32),
            VMEM((2, NY, TILE, F), f32),
            VMEM((2, NY, TILE, F), f32),
            VMEM((2, NY, TILE, F), bf16),
            VMEM((2, NY, TILE, F), bf16),
            dma((10,)),
            dma((1 + HUB_ITEM,)),
            dma((2, ROWS)),
            dma((2, ROWS)),
            dma((CLASS,)),
            dma((CLASS,)),
            dma((HUB_ITEM,)),
            dma((HUB_ITEM,)),
            dma((HUB_ITEM,)),
            dma((HUB_ITEM,)),
            dma((HUB_ITEM + 1, 8)),
            dma((HUB_ITEM + 1, 8)),
            dma((HUB_ITEM + 1, 9)),
            dma((HUB_ITEM + 1, 9)),
            dma((HUB_ITEM, NX)),
            dma((HUB_ITEM, NX)),
            dma((2, NY)),
            dma((2, NY)),
            dma((2, NY)),
            dma((2, NY)),
        ],
        compiler_params=pltpu.CompilerParams(
            collective_id=0, has_side_effects=True, vmem_limit_bytes=56 * 1024 * 1024
        ),
        name="layer",
    )(
        features.reshape(ROWS, TILE, F), hub_local, picks, rows_in,
        tile_slots.reshape(1, KT), tile_values[0, 0], weight, out_bias.reshape(1, F),
    )


def solution(mesh):
    placed = (
        P("row", None),
        P("row", None),
        P("row", "rep", None, None),
        P("row", "rep", None),
        P("row", "rep", None),
        P("row", "rep", None, None, None),
        P(),
        P(),
    )
    return jax.shard_map(
        local, mesh=mesh, in_specs=placed, out_specs=P(("row", "rep"), None), check_vma=False
    )
```

time: 77.1 us -> 74.1 us (0.961)
  Pallas kernels: 74.7 us -> 71.8 us
    pallas_call x1, Pallas kernels: 74.7 us -> 71.8 us  [local(): pl.pallas_call(layer_kernel, out_shape=jax.ShapeDtypeStruct((SHARE, F), b...]
where the time goes in v4:
time: 74.1 us; the launch traced here: 73.9 us
  Pallas kernels  71.8 us (97%)
  local copies, waits for them, and re-layouts  1.47 us (2%)
    pallas_call x1, Pallas kernels, local(): pl.pallas_call(layer_kernel, out_shape=jax.ShapeDtypeStruct((SHARE, F), b...  71.8 us

profile of v4, /device:TPU:1, one launch (start us, length us, event | category | flops | bytes accessed | tf_op | source)
XLA Modules:
  0.0 73.9 jit_solution(14090521611214080722)
XLA Ops:
  0.7 71.8 %layer.1 = bf16[256,128]{1,0:T(8,128)(2,1)} custom-call(bf16[32,128,128]{2,1,0:T(8,128)(2,1)} %bitcast.9, s32[1,1]{1,0:T(1,128)S(6)} %copy.10.hub_in, s32[2,32]{1,0:T(2,128)} %bitcast.10, s32[1,112]{1,0:T(1,128)} %bitcast.11, s32[1,112]{1,0:T(1,128)} %bitcast.12, bf16[112,128,128]{2,1,0:T(8,128)(2,1)} %bitcast.8, bf16[128,128]{1,0:T(8,128)(2,1)} %weight_in.1, ...), custom_call_target="tpu_custom_call" | custom-call | tf_op jit(solution)/shard_map/layer/pallas_call | solution.py:396
  72.5 1.5 %copy.11 = bf16[256,128]{1,0:T(8,128)(2,1)} copy(bf16[256,128]{1,0:T(8,128)(2,1)} %layer.1) | data formatting | bytes 131072

commit v5 on v4

--- a/solution.py
+++ b/solution.py
@@ -32,7 +32,7 @@
 SHARE = 256
 HALF = F // 2
 ORDER = tuple(zigzag(k, NY // 2) for k in range(NY))
-UNROLL = 28
+UNROLL = 56
 
 
 def halves(one, two):

time: 74.1 us -> 73.7 us (level)
  no operation moved by 1% of the time
where the time goes in v5:
time: 73.7 us; the launch traced here: 73.5 us
  Pallas kernels  71.4 us (97%)
  local copies, waits for them, and re-layouts  1.47 us (2%)
    pallas_call x1, Pallas kernels, local(): pl.pallas_call(layer_kernel, out_shape=jax.ShapeDtypeStruct((SHARE, F), b...  71.4 us

profile of v5, /device:TPU:1, one launch (start us, length us, event | category | flops | bytes accessed | tf_op | source)
XLA Modules:
  0.0 73.5 jit_solution(13396785072089231309)
XLA Ops:
  0.7 71.4 %layer.1 = bf16[256,128]{1,0:T(8,128)(2,1)} custom-call(bf16[32,128,128]{2,1,0:T(8,128)(2,1)} %bitcast.9, s32[1,1]{1,0:T(1,128)S(6)} %copy.10.hub_in, s32[2,32]{1,0:T(2,128)} %bitcast.10, s32[1,112]{1,0:T(1,128)} %bitcast.11, s32[1,112]{1,0:T(1,128)} %bitcast.12, bf16[112,128,128]{2,1,0:T(8,128)(2,1)} %bitcast.8, bf16[128,128]{1,0:T(8,128)(2,1)} %weight_in.1, ...), custom_call_target="tpu_custom_call" | custom-call | tf_op jit(solution)/shard_map/layer/pallas_call | solution.py:396
  72.1 1.5 %copy.11 = bf16[256,128]{1,0:T(8,128)(2,1)} copy(bf16[256,128]{1,0:T(8,128)(2,1)} %layer.1) | data formatting | bytes 131072
